TPU v7x, 32 devices: a whole 2x2x4 slice. The times are simulated.
32 devices in a mesh: shot: 4 (over y, x), mp: 8 (over z, core).
Axes of the slice: x: 2, y: 2, z: 4, core: 2. Of those that a mesh axis runs over, the one named last changes fastest.
Arguments:
- courant: float32 [2, 128, 64, 256], P(None, 'mp'), may hold values from 0.05 to 0.2
- aperture_first: int32 [4], P('shot'), may hold values from 0 to 8
- source_pos: int32 [4, 3], P('shot'), may hold values from 0 to 255, as said below
- wavelet: float32 [4, 4], P('shot'), may hold values from -6 to 6
- receiver_pos: int32 [4, 32, 3], P('shot'), may hold values from 0 to 255, as said below
- residual: float32 [4, 4, 32], P('shot'), may hold values from -6 to 6
- step_count: int32 [4], P('shot'), may hold values from 2 to 4
- forward_prev: float32 [4, 128, 64, 256], P('shot', 'mp'), may hold values from -1 to 1
- forward_now: float32 [4, 128, 64, 256], P('shot', 'mp'), may hold values from -1 to 1
- adjoint_prev: float32 [4, 128, 64, 256], P('shot', 'mp'), may hold values from -1 to 1
- adjoint_now: float32 [4, 128, 64, 256], P('shot', 'mp'), may hold values from -1 to 1
Outputs:
- gradient: float32 [2, 128, 64, 256], P(None, 'mp', 'shot')
Inputs may be any that keep to these rules, and one draw needn't show every extreme that they name: `source_pos`: each component lies inside the aperture grid: first in 0..127, second in 0..63, third in 0..255. `receiver_pos`: each component lies inside the aperture grid (first in 0..127, second in 0..63, third in 0..255), within 12 cells of the shot's source along every dimension. The aperture covers model tiles aperture_first .. aperture_first + 7.
All inputs are finite; a program needn't handle non-finite values.
Results may differ from a plain program's by a relative error of at most 0.0003.
Values sent between devices are 32-bit elements; how exact they have to be, the bound alone decides.
A program may use at most 128 MiB of HBM per device.

v0:
```python
import jax
import jax.numpy as jnp
from jax import lax
from jax.sharding import PartitionSpec as P

COEF = (-205.0 / 72.0, 1.6, -0.2, 8.0 / 315.0, -1.0 / 560.0)


def extended(value, sides, width):
    for axis, dim in sides:
        size, length = (lax.axis_size(axis), value.shape[dim])
        up = [(i, (i + 1) % size) for i in range(size - 1)]
        down = [(j, i) for i, j in up]
        last = lax.slice_in_dim(value, length - width, length, axis=dim)
        leading = lax.slice_in_dim(value, 0, width, axis=dim)
        before = lax.ppermute(last, axis, up)
        after = lax.ppermute(leading, axis, down)
        value = jnp.concatenate([before, value, after], axis=dim)
    return value


def passed_along(value, axis, steps):
    count = lax.axis_size(axis)
    pairs = [(source, (source + steps) % count) for source in range(count)]
    return lax.ppermute(value, axis, pairs)


def laplace_core(padded, width):
    ys = padded.shape[2]
    zs = padded.shape[3]
    centre = padded[:, 4 : 4 + width]
    side = jnp.pad(centre, ((0, 0), (0, 0), (4, 4), (4, 4)))
    total = 3.0 * COEF[0] * centre
    for k in range(1, 5):
        total = total + COEF[k] * (
            padded[:, 4 + k : 4 + k + width] + padded[:, 4 - k : 4 - k + width]
        )
        total = total + COEF[k] * (
            side[:, :, 4 + k : 4 + k + ys, 4 : 4 + zs] + side[:, :, 4 - k : 4 - k + ys, 4 : 4 + zs]
        )
        total = total + COEF[k] * (
            side[:, :, 4 : 4 + ys, 4 + k : 4 + k + zs] + side[:, :, 4 : 4 + ys, 4 - k : 4 - k + zs]
        )
    return total


def laplace(field):
    width = field.shape[1]
    padded = extended(field, (("mp", 1),), 4)
    return laplace_core(padded, width)


def body(
    courant,
    aperture_first,
    source_pos,
    wavelet,
    receiver_pos,
    residual,
    step_count,
    forward_prev,
    forward_now,
    adjoint_prev,
    adjoint_now,
):
    tile_x = courant.shape[1]
    ny_cells = courant.shape[2]
    nz_cells = courant.shape[3]
    mp_size = lax.axis_size("mp")
    bit_count = mp_size.bit_length() - 1
    me_index = lax.axis_index("mp")
    first = aperture_first[0]
    owned = jnp.where(me_index < first, courant[1], courant[0])
    for bit in range(bit_count):
        moved = passed_along(owned, "mp", mp_size - (1 << bit))
        owned = jnp.where((first >> bit) % 2 == 1, moved, owned)
    steps = wavelet.shape[1]
    margin = 0
    u_prev, u_now = (forward_prev, forward_now)
    w_prev, w_now = (adjoint_prev, adjoint_now)
    width = tile_x + 2 * margin
    x_base = me_index * tile_x - margin
    x_cells = jnp.arange(width, dtype=jnp.int32) + x_base
    y_cells = jnp.arange(ny_cells, dtype=jnp.int32)
    z_cells = jnp.arange(nz_cells, dtype=jnp.int32)
    src_x = (x_cells[None, :] == source_pos[:, 0:1]).astype(jnp.float32)
    src_y = (y_cells[None, :] == source_pos[:, 1:2]).astype(jnp.float32)
    src_z = (z_cells[None, :] == source_pos[:, 2:3]).astype(jnp.float32)
    src_field = src_x[:, :, None, None] * (src_y[:, :, None] * src_z[:, None, :])[:, None, :, :]
    rec_x = (x_cells[None, None, :] == receiver_pos[:, :, 0:1]).astype(jnp.float32)
    rec_y = (y_cells[None, None, :] == receiver_pos[:, :, 1:2]).astype(jnp.float32)
    rec_z = (z_cells[None, None, :] == receiver_pos[:, :, 2:3]).astype(jnp.float32)
    rec_plane = rec_y[:, :, :, None] * rec_z[:, :, None, :]
    stored = []
    for n in range(steps):
        drive = laplace(u_now) + wavelet[:, n][:, None, None, None] * src_field
        u_next = 2.0 * u_now - u_prev + owned[None] * drive
        active = (n < step_count)[:, None, None, None]
        stored.append(jnp.where(active, drive, 0.0))
        u_prev, u_now = (jnp.where(active, u_now, u_prev), jnp.where(active, u_next, u_now))
    image = jnp.zeros((width, ny_cells, nz_cells), jnp.float32)
    for k in range(steps):
        n = steps - 1 - k
        weighted = rec_x * residual[:, n, :][:, :, None]
        inject = jnp.einsum("srx,sryz->sxyz", weighted, rec_plane, precision=lax.Precision.HIGHEST)
        w_next = 2.0 * w_now - w_prev + owned[None] * (laplace(w_now) + inject)
        active = (n < step_count)[:, None, None, None]
        image = image + jnp.sum(jnp.where(active, w_next * stored[n], 0.0), axis=0)
        w_prev, w_now = (jnp.where(active, w_now, w_prev), jnp.where(active, w_next, w_now))
    returned = image
    for bit in range(bit_count):
        moved = passed_along(returned, "mp", 1 << bit)
        returned = jnp.where((first >> bit) % 2 == 1, moved, returned)
    blank = jnp.zeros_like(returned)
    both_rows = jnp.where(
        me_index < first, jnp.stack([blank, returned]), jnp.stack([returned, blank])
    )
    return lax.psum_scatter(both_rows, "shot", scatter_dimension=2, tiled=True)


def solution(mesh):
    return jax.shard_map(
        body,
        mesh=mesh,
        in_specs=(
            P(None, "mp", None, None),
            P("shot"),
            P("shot", None),
            P("shot", None),
            P("shot", None, None),
            P("shot", None, None),
            P("shot"),
            P("shot", "mp", None, None),
            P("shot", "mp", None, None),
            P("shot", "mp", None, None),
            P("shot", "mp", None, None),
        ),
        out_specs=P(None, "mp", "shot", None),
        check_vma=False,
    )
```

profile of v0, /device:TPU:0, one launch (start us, length us, event | category | flops | bytes accessed | tf_op | source)
XLA Modules:
  0.0 360.2 jit_solution(312852852139599700)
XLA Ops:
  7.2 1.7 fusion.455
  8.9 2.1 fusion.407
  11.0 4.5 %collective-permute-start = (f32[16,64,256]{2,0,1:T(8,128)}, f32[16,64,256]{2,0,1:T(8,128)}, u32[]{:S(2)}, u32[]{:S(2)}) collective-permute-start(f32[16,64,256]{2,0,1:T(8,128)} %fusion.407), channel_id=1, source_target_pairs={{0,7},{1,0},{2,1},{3,2},{4,3},{5,4},{6,5},{7,6},{8,15},{9,8},{10,9... | collective-permute-start | bytes 3145736 | tf_op jit(solution)/shard_map/ppermute | solution.py:25
  19.3 3.0 collective-permute-start.6
  23.1 4.1 %copy_select_fusion.2 = (f32[1,16,64,256]{3,1,2,0:T(8,128)}, f32[1,20,64,256]{3,1,2,0:T(8,128)}, f32[1,16,64,256]{3,1,2,0:T(8,128)S(1)}) fusion(f32[1,16,64,256]{3,2,1,0:T(8,128)} %param.20, pred[]{:T(512)} %bitcast.1, f32[1,16,64,256]{3,2,1,0:T(8,128)} %param.21), kind=kLoop, calls=%fused_computation.620 | loop fusion | flops 262143 | bytes 5242881 | tf_op jit(solution)/shard_map/jit(_where)/select_n | solution.py:109
  27.2 3.8 %collective-permute-done = f32[16,64,256]{2,0,1:T(8,128)} collective-permute-done((f32[16,64,256]{2,0,1:T(8,128)}, f32[16,64,256]{2,0,1:T(8,128)}, u32[]{:S(2)}, u32[]{:S(2)}) %collective-permute-start) | collective-permute-done | bytes 1048608 | tf_op jit(solution)/shard_map/ppermute | solution.py:25
  31.0 2.4 broadcast_select_fusion.5
  35.5 7.1 %collective-permute-start.4 = (f32[1,4,64,256]{3,1,2,0:T(4,128)}, f32[1,4,64,256]{3,1,2,0:T(4,128)}, u32[]{:S(2)}, u32[]{:S(2)}) collective-permute-start(f32[1,4,64,256]{3,1,2,0:T(4,128)} %get-tuple-element.34), channel_id=1, source_target_pairs={{0,1},{1,2},{2,3},{3,4},{4,5},{5,6},{6,7},{8,9},{9,10},{10,11},{11... | collective-permute-start | bytes 786440 | tf_op jit(solution)/shard_map/ppermute | solution.py:16
  44.7 10.7 %collective-permute-done.1 = f32[16,64,256]{2,0,1:T(8,128)} collective-permute-done((f32[16,64,256]{2,0,1:T(8,128)}, f32[16,64,256]{2,0,1:T(8,128)}, u32[]{:S(2)}, u32[]{:S(2)}) %collective-permute-start.1) | collective-permute-done | bytes 1048608 | tf_op jit(solution)/shard_map/ppermute | solution.py:25
  55.4 2.4 broadcast_select_fusion.7
  61.2 46.0 %collective-permute-done.2 = f32[16,64,256]{2,0,1:T(8,128)} collective-permute-done((f32[16,64,256]{2,0,1:T(8,128)}, f32[16,64,256]{2,0,1:T(8,128)}, u32[]{:S(2)}, u32[]{:S(2)}) %collective-permute-start.2) | collective-permute-done | bytes 1048608 | tf_op jit(solution)/shard_map/ppermute | solution.py:25
  107.2 16.1 %fusion.409 = (f32[1,16,64,256]{3,1,2,0:T(8,128)S(1)}, f32[1,16,64,256]{3,1,2,0:T(8,128)S(1)}, f32[16,64,256]{2,0,1:T(8,128)S(1)}) fusion(f32[1,16,64,256]{3,2,1,0:T(8,128)S(1)} %copy-done.1, pred[]{:T(512)} %bitcast.12, f32[1,16,64,256]{3,2,1,0:T(8,128)S(1)} %copy-done, f32[64,256]{1,0:T(8,128)S(1)} %broadcast_multiply_fusion, ...), kind=kLoop, calls=%fused_computation.604 | loop fusion | flops 13107200 | bytes 12910662 | tf_op jit(solution)/shard_map/jit(_where)/select_n | solution.py:100
  124.7 3.0 collective-permute-start.8
  127.8 9.7 %broadcast_select_fusion.3 = (f32[1,16,64,256]{3,1,2,0:T(8,128)S(1)}, f32[1,16,64,256]{3,1,2,0:T(8,128)}) fusion(pred[]{:T(512)} %bitcast.1, f32[1,16,64,256]{3,2,1,0:T(8,128)S(1)} %copy-done.5, f32[32,256]{1,0:T(8,128)S(1)} %fusion.423, f32[32,64]{0,1:T(8,128)S(1)} %fusion.422, f32[32]{0:T(128)S(1)} %copy-done.19, s32[32]{0:T(128)S(1)} %get-tuple-element.39, ...), kind=kOutput, calls=%fused_computation.624 | convolution fusion | flops 113509376 | bytes 10789185 | tf_op jit(solution)/shard_map/srx,sryz->sxyz/dot_general | solution.py:105
  138.9 4.6 %collective-permute-start.14 = (f32[1,4,64,256]{3,1,2,0:T(4,128)S(1)}, f32[1,4,64,256]{3,1,2,0:T(4,128)}, u32[]{:S(2)}, u32[]{:S(2)}) collective-permute-start(f32[1,4,64,256]{3,1,2,0:T(4,128)S(1)} %get-tuple-element.28), channel_id=1, source_target_pairs={{0,1},{1,2},{2,3},{3,4},{4,5},{5,6},{6,7},{8,9},{9,10},{10,11},{11... | collective-permute-start | bytes 786440 | tf_op jit(solution)/shard_map/ppermute | solution.py:16
  144.3 7.7 %fusion.411 = (f32[1,16,64,256]{3,1,2,0:T(8,128)S(1)}, f32[1,16,64,256]{3,1,2,0:T(8,128)S(1)}) fusion(f32[16,64,256]{2,0,1:T(8,128)S(1)} %get-tuple-element.11, pred[]{:T(512)} %bitcast.11, f32[1,16,64,256]{3,2,1,0:T(8,128)S(1)} %copy-done.1, pred[]{:T(512)} %bitcast.12, f32[1,16,64,256]{3,1,2,0:T(8,128)S(1)} %get-tuple-element.10, ...), kind=kLoop, calls=%fused_computation.606 | loop fusion | flops 15466496 | bytes 7929926 | tf_op jit(solution)/shard_map/jit(_where)/select_n | solution.py:100
  152.1 1.3 collective-permute-start.9
  153.4 3.8 %collective-permute-start.10 = (f32[1,4,64,256]{3,1,2,0:T(4,128)S(1)}, f32[1,4,64,256]{3,1,2,0:T(4,128)S(1)}, u32[]{:S(2)}, u32[]{:S(2)}) collective-permute-start(f32[1,4,64,256]{3,1,2,0:T(4,128)S(1)} %get-tuple-element.19), channel_id=1, source_target_pairs={{0,1},{1,2},{2,3},{3,4},{4,5},{5,6},{6,7},{8,9},{9,10},{10,11},{11... | collective-permute-start | bytes 786440 | tf_op jit(solution)/shard_map/ppermute | solution.py:16
  157.2 6.4 %broadcast_select_fusion.1 = (f32[1,16,64,256]{3,1,2,0:T(8,128)S(1)}, f32[1,16,64,256]{3,1,2,0:T(8,128)}) fusion(f32[1,16,64,256]{3,1,2,0:T(8,128)S(1)} %copy-done.10, pred[]{:T(512)} %bitcast.10, f32[32,256]{1,0:T(8,128)S(1)} %fusion.423, f32[32,64]{0,1:T(8,128)S(1)} %fusion.422, f32[32]{0:T(128)S(1)} %copy-done.18, s32[32]{0:T(128)S(1)} %get-tuple-element.39, ...), kind=kOutput, calls=%fused_computation.622 | convolution fusion | flops 114557952 | bytes 5808449 | tf_op jit(solution)/shard_map/srx,sryz->sxyz/dot_general | solution.py:105
  165.9 5.0 %collective-permute-start.16 = (f32[1,4,64,256]{3,1,2,0:T(4,128)}, f32[1,4,64,256]{3,1,2,0:T(4,128)}, u32[]{:S(2)}, u32[]{:S(2)}) collective-permute-start(f32[1,4,64,256]{3,1,2,0:T(4,128)} %get-tuple-element.23), channel_id=1, source_target_pairs={{0,1},{1,2},{2,3},{3,4},{4,5},{5,6},{6,7},{8,9},{9,10},{10,11},{11... | collective-permute-start | bytes 786440 | tf_op jit(solution)/shard_map/ppermute | solution.py:16
  171.6 7.6 %fusion.413 = (f32[1,16,64,256]{3,1,2,0:T(8,128)S(1)}, f32[1,16,64,256]{3,1,2,0:T(8,128)S(1)}) fusion(f32[16,64,256]{2,0,1:T(8,128)S(1)} %get-tuple-element.11, f32[1,16,64,256]{3,1,2,0:T(8,128)S(1)} %get-tuple-element.8, pred[]{:T(512)} %bitcast.11, pred[]{:T(512)} %bitcast.10, f32[1,16,64,256]{3,2,1,0:T(8,128)S(1)} %copy-done.1, pred[]{:T(512)} %bitcast.12, ...), kind=kLoop, calls=%fused_computation.608 | loop fusion | flops 17039360 | bytes 8978503 | tf_op jit(solution)/shard_map/jit(_where)/select_n | solution.py:100
  180.6 3.6 %collective-permute-start.12 = (f32[1,4,64,256]{3,1,2,0:T(4,128)S(1)}, f32[1,4,64,256]{3,1,2,0:T(4,128)S(1)}, u32[]{:S(2)}, u32[]{:S(2)}) collective-permute-start(f32[1,4,64,256]{3,1,2,0:T(4,128)S(1)} %get-tuple-element.15), channel_id=1, source_target_pairs={{0,1},{1,2},{2,3},{3,4},{4,5},{5,6},{6,7},{8,9},{9,10},{10,11},{11... | collective-permute-start | bytes 786440 | tf_op jit(solution)/shard_map/ppermute | solution.py:16
  184.3 17.5 %broadcast_select_fusion = (f32[1,16,64,256]{3,1,2,0:T(8,128)S(1)}, f32[1,16,64,256]{3,1,2,0:T(8,128)}) fusion(f32[1,16,64,256]{3,1,2,0:T(8,128)} %copy-done.12, pred[]{:T(512)} %bitcast.11, f32[32,256]{1,0:T(8,128)S(1)} %fusion.423, f32[32,64]{0,1:T(8,128)S(1)} %fusion.422, f32[32]{0:T(128)S(1)} %get-tuple-element.38, s32[32]{0:T(128)S(1)} %get-tuple-element.39, ...), kind=kOutput, calls=%fused_computation.621 | convolution fusion | flops 114820096 | bytes 6857026 | tf_op jit(solution)/shard_map/srx,sryz->sxyz/dot_general | solution.py:105
  203.2 4.3 %collective-permute-start.18 = (f32[1,4,64,256]{3,1,2,0:T(4,128)S(1)}, f32[1,4,64,256]{3,1,2,0:T(4,128)S(1)}, u32[]{:S(2)}, u32[]{:S(2)}) collective-permute-start(f32[1,4,64,256]{3,1,2,0:T(4,128)S(1)} %get-tuple-element.17), channel_id=1, source_target_pairs={{0,1},{1,2},{2,3},{3,4},{4,5},{5,6},{6,7},{8,9},{9,10},{10,11},{11... | collective-permute-start | bytes 786440 | tf_op jit(solution)/shard_map/ppermute | solution.py:16
  209.3 11.6 %fusion.38 = f32[16,64,256]{2,0,1:T(8,128)S(1)} fusion(f32[1,16,64,256]{3,1,2,0:T(8,128)S(1)} %get-tuple-element.53, f32[1,16,64,256]{3,1,2,0:T(8,128)} %get-tuple-element.50, f32[1,16,64,256]{3,1,2,0:T(8,128)S(1)} %get-tuple-element.5, f32[1,4,64,256]{3,1,2,0:T(4,128)} %copy-done.22, f32[1,4,64,256]{3,1,2,0:T(4,128)} %copy-done.21, ...), kind=kOutput, calls=%fused_computation.235 | convolution fusion | flops 131335168 | bytes 14786952 | tf_op jit(solution)/shard_map/srx,sryz->sxyz/dot_general | solution.py:105
  220.9 3.9 %collective-permute-start.19 = (f32[16,64,256]{2,0,1:T(8,128)S(1)}, f32[16,64,256]{2,0,1:T(8,128)S(1)}, u32[]{:S(2)}, u32[]{:S(2)}) collective-permute-start(f32[16,64,256]{2,0,1:T(8,128)S(1)} %fusion.38), channel_id=1, source_target_pairs={{0,1},{1,2},{2,3},{3,4},{4,5},{5,6},{6,7},{7,0},{8,9},{9,10},{10,1... | collective-permute-start | bytes 3145736 | tf_op jit(solution)/shard_map/ppermute | solution.py:25
  224.9 12.1 %collective-permute-done.19 = f32[16,64,256]{2,0,1:T(8,128)S(1)} collective-permute-done((f32[16,64,256]{2,0,1:T(8,128)S(1)}, f32[16,64,256]{2,0,1:T(8,128)S(1)}, u32[]{:S(2)}, u32[]{:S(2)}) %collective-permute-start.19) | collective-permute-done | bytes 1048608 | tf_op jit(solution)/shard_map/ppermute | solution.py:25
  237.2 4.7 %collective-permute-start.20 = (f32[16,64,256]{2,0,1:T(8,128)S(1)}, f32[16,64,256]{2,0,1:T(8,128)S(1)}, u32[]{:S(2)}, u32[]{:S(2)}) collective-permute-start(f32[16,64,256]{2,0,1:T(8,128)S(1)} %broadcast_select_fusion.4), channel_id=1, source_target_pairs={{0,2},{1,3},{2,4},{3,5},{4,6},{5,7},{6,0},{7,1},{8,10},{9,11},{10,... | collective-permute-start | bytes 3145736 | tf_op jit(solution)/shard_map/ppermute | solution.py:25
  241.9 24.2 %collective-permute-done.20 = f32[16,64,256]{2,0,1:T(8,128)S(1)} collective-permute-done((f32[16,64,256]{2,0,1:T(8,128)S(1)}, f32[16,64,256]{2,0,1:T(8,128)S(1)}, u32[]{:S(2)}, u32[]{:S(2)}) %collective-permute-start.20) | collective-permute-done | bytes 1048608 | tf_op jit(solution)/shard_map/ppermute | solution.py:25
  266.4 45.6 %collective-permute-done.21 = f32[16,64,256]{2,0,1:T(8,128)S(1)} collective-permute-done((f32[16,64,256]{2,0,1:T(8,128)S(1)}, f32[16,64,256]{2,0,1:T(8,128)S(1)}, u32[]{:S(2)}, u32[]{:S(2)}) %collective-permute-start.21) | collective-permute-done | bytes 1048608 | tf_op jit(solution)/shard_map/ppermute | solution.py:25
  312.8 2.5 copy.67
  315.4 35.6 %reduce-scatter.5.cloned.1.call-done = f32[16,8192]{1,0:T(8,128)} async-done(((f32[64,8192]{1,0:T(8,128)}), f32[16,8192]{1,0:T(8,128)}) %reduce-scatter.5.cloned.1.call-update) | async-done | bytes 524304
  (105 shorter events, 26.0 us)
Async XLA Ops:
  6.5 344.5 %reduce-scatter.5.cloned.1.call-start = ((), (), s32[]{:S(2)}) async-start(), calls=%async_computation.1 | async-start | bytes 2621440
  11.0 19.9 %collective-permute-start = (f32[16,64,256]{2,0,1:T(8,128)}, f32[16,64,256]{2,0,1:T(8,128)}, u32[]{:S(2)}, u32[]{:S(2)}) collective-permute-start(f32[16,64,256]{2,0,1:T(8,128)} %fusion.407), channel_id=1, source_target_pairs={{0,7},{1,0},{2,1},{3,2},{4,3},{5,4},{6,5},{7,6},{8,15},{9,8},{10,9... | collective-permute-start | bytes 3145736 | tf_op jit(solution)/shard_map/ppermute | solution.py:25
  18.0 42.2 %collective-permute-start.5 = (f32[1,4,64,256]{3,1,2,0:T(4,128)}, f32[1,4,64,256]{3,1,2,0:T(4,128)S(1)}, u32[]{:S(2)}, u32[]{:S(2)}) collective-permute-start(f32[1,4,64,256]{3,1,2,0:T(4,128)} %get-tuple-element.29), channel_id=1, source_target_pairs={{1,0},{2,1},{3,2},{4,3},{5,4},{6,5},{7,6},{9,8},{10,9},{11,10},{12... | collective-permute-start | bytes 786440 | tf_op jit(solution)/shard_map/ppermute | solution.py:17
  19.3 41.8 %collective-permute-start.6 = (f32[1,4,64,256]{3,1,2,0:T(4,128)}, f32[1,4,64,256]{3,1,2,0:T(4,128)S(1)}, u32[]{:S(2)}, u32[]{:S(2)}) collective-permute-start(f32[1,4,64,256]{3,1,2,0:T(4,128)} %get-tuple-element.30), channel_id=1, source_target_pairs={{0,1},{1,2},{2,3},{3,4},{4,5},{5,6},{6,7},{8,9},{9,10},{10,11},{11... | collective-permute-start | bytes 786440 | tf_op jit(solution)/shard_map/ppermute | solution.py:16
  27.2 16.8 %copy-start.17 = (s32[1,32,3]{1,0,2:T(1,128)S(1)}, s32[1,32,3]{1,0,2:T(1,128)}, u32[]{:S(2)}) copy-start(s32[1,32,3]{1,0,2:T(1,128)} %param.15) | copy-start | bytes 1156
  27.2 16.8 %copy-start.16 = (f32[1,4,32]{2,1,0:T(4,128)S(1)}, f32[1,4,32]{2,1,0:T(4,128)}, u32[]{:S(2)}) copy-start(f32[1,4,32]{2,1,0:T(4,128)} %param.16) | copy-start | bytes 1540
  33.4 22.0 %collective-permute-start.1 = (f32[16,64,256]{2,0,1:T(8,128)}, f32[16,64,256]{2,0,1:T(8,128)}, u32[]{:S(2)}, u32[]{:S(2)}) collective-permute-start(f32[16,64,256]{2,0,1:T(8,128)} %broadcast_select_fusion.5), channel_id=1, source_target_pairs={{0,6},{1,7},{2,0},{3,1},{4,2},{5,3},{6,4},{7,5},{8,14},{9,15},{10,... | collective-permute-start | bytes 3145736 | tf_op jit(solution)/shard_map/ppermute | solution.py:25
  34.2 26.1 %collective-permute-start.3 = (f32[1,4,64,256]{3,1,2,0:T(4,128)}, f32[1,4,64,256]{3,1,2,0:T(4,128)S(1)}, u32[]{:S(2)}, u32[]{:S(2)}) collective-permute-start(f32[1,4,64,256]{3,1,2,0:T(4,128)} %get-tuple-element.33), channel_id=1, source_target_pairs={{1,0},{2,1},{3,2},{4,3},{5,4},{6,5},{7,6},{9,8},{10,9},{11,10},{12... | collective-permute-start | bytes 786440 | tf_op jit(solution)/shard_map/ppermute | solution.py:17
  35.5 92.2 %collective-permute-start.4 = (f32[1,4,64,256]{3,1,2,0:T(4,128)}, f32[1,4,64,256]{3,1,2,0:T(4,128)}, u32[]{:S(2)}, u32[]{:S(2)}) collective-permute-start(f32[1,4,64,256]{3,1,2,0:T(4,128)} %get-tuple-element.34), channel_id=1, source_target_pairs={{0,1},{1,2},{2,3},{3,4},{4,5},{5,6},{6,7},{8,9},{9,10},{10,11},{11... | collective-permute-start | bytes 786440 | tf_op jit(solution)/shard_map/ppermute | solution.py:16
  57.7 49.4 %collective-permute-start.2 = (f32[16,64,256]{2,0,1:T(8,128)}, f32[16,64,256]{2,0,1:T(8,128)}, u32[]{:S(2)}, u32[]{:S(2)}) collective-permute-start(f32[16,64,256]{2,0,1:T(8,128)} %broadcast_select_fusion.7), channel_id=1, source_target_pairs={{0,4},{1,5},{2,6},{3,7},{4,0},{5,1},{6,2},{7,3},{8,12},{9,13},{10,... | collective-permute-start | bytes 3145736 | tf_op jit(solution)/shard_map/ppermute | solution.py:25
  60.3 46.9 %copy-start.1 = (f32[1,16,64,256]{3,2,1,0:T(8,128)S(1)}, f32[1,16,64,256]{3,2,1,0:T(8,128)}, u32[]{:S(2)}) copy-start(f32[1,16,64,256]{3,2,1,0:T(8,128)} %param.18) | copy-start | bytes 3145732
  107.1 20.6 %copy-start.4 = (f32[1,16,64,256]{3,1,2,0:T(8,128)S(1)}, f32[1,16,64,256]{3,1,2,0:T(8,128)}, u32[]{:S(2)}) copy-start(f32[1,16,64,256]{3,1,2,0:T(8,128)} %copy-done.3) | copy-start | bytes 3145732
  107.1 20.6 %copy-start.5 = (f32[1,16,64,256]{3,2,1,0:T(8,128)S(1)}, f32[1,16,64,256]{3,2,1,0:T(8,128)}, u32[]{:S(2)}) copy-start(f32[1,16,64,256]{3,2,1,0:T(8,128)} %param.21) | copy-start | bytes 3145732
  107.1 20.6 %copy-start.19 = (f32[32]{0:T(128)S(1)}, f32[32]{0:T(128)}, u32[]{:S(2)}) copy-start(f32[32]{0:T(128)} %get-tuple-element.37) | copy-start | bytes 388
  107.2 20.6 %copy-start.23 = (s32[16]{0:T(128)S(1)}, s32[16]{0:T(128)}, u32[]{:S(2)}) copy-start(s32[16]{0:T(128)} %iota_add_fusion) | copy-start | bytes 196
  123.4 20.2 %collective-permute-start.7 = (f32[1,4,64,256]{3,1,2,0:T(4,128)S(1)}, f32[1,4,64,256]{3,1,2,0:T(4,128)S(1)}, u32[]{:S(2)}, u32[]{:S(2)}) collective-permute-start(f32[1,4,64,256]{3,1,2,0:T(4,128)S(1)} %get-tuple-element.20), channel_id=1, source_target_pairs={{1,0},{2,1},{3,2},{4,3},{5,4},{6,5},{7,6},{9,8},{10,9},{11,10},{12... | collective-permute-start | bytes 786440 | tf_op jit(solution)/shard_map/ppermute | solution.py:17
  124.7 18.9 %collective-permute-start.8 = (f32[1,4,64,256]{3,1,2,0:T(4,128)S(1)}, f32[1,4,64,256]{3,1,2,0:T(4,128)S(1)}, u32[]{:S(2)}, u32[]{:S(2)}) collective-permute-start(f32[1,4,64,256]{3,1,2,0:T(4,128)S(1)} %get-tuple-element.21), channel_id=1, source_target_pairs={{0,1},{1,2},{2,3},{3,4},{4,5},{5,6},{6,7},{8,9},{9,10},{10,11},{11... | collective-permute-start | bytes 786440 | tf_op jit(solution)/shard_map/ppermute | solution.py:16
  137.6 19.5 %collective-permute-start.13 = (f32[1,4,64,256]{3,1,2,0:T(4,128)S(1)}, f32[1,4,64,256]{3,1,2,0:T(4,128)S(1)}, u32[]{:S(2)}, u32[]{:S(2)}) collective-permute-start(f32[1,4,64,256]{3,1,2,0:T(4,128)S(1)} %get-tuple-element.27), channel_id=1, source_target_pairs={{1,0},{2,1},{3,2},{4,3},{5,4},{6,5},{7,6},{9,8},{10,9},{11,10},{12... | collective-permute-start | bytes 786440 | tf_op jit(solution)/shard_map/ppermute | solution.py:17
  138.9 18.2 %collective-permute-start.14 = (f32[1,4,64,256]{3,1,2,0:T(4,128)S(1)}, f32[1,4,64,256]{3,1,2,0:T(4,128)}, u32[]{:S(2)}, u32[]{:S(2)}) collective-permute-start(f32[1,4,64,256]{3,1,2,0:T(4,128)S(1)} %get-tuple-element.28), channel_id=1, source_target_pairs={{0,1},{1,2},{2,3},{3,4},{4,5},{5,6},{6,7},{8,9},{9,10},{10,11},{11... | collective-permute-start | bytes 786440 | tf_op jit(solution)/shard_map/ppermute | solution.py:16
  152.1 18.8 %collective-permute-start.9 = (f32[1,4,64,256]{3,1,2,0:T(4,128)S(1)}, f32[1,4,64,256]{3,1,2,0:T(4,128)S(1)}, u32[]{:S(2)}, u32[]{:S(2)}) collective-permute-start(f32[1,4,64,256]{3,1,2,0:T(4,128)S(1)} %get-tuple-element.18), channel_id=1, source_target_pairs={{1,0},{2,1},{3,2},{4,3},{5,4},{6,5},{7,6},{9,8},{10,9},{11,10},{12... | collective-permute-start | bytes 786440 | tf_op jit(solution)/shard_map/ppermute | solution.py:17
  153.4 17.5 %collective-permute-start.10 = (f32[1,4,64,256]{3,1,2,0:T(4,128)S(1)}, f32[1,4,64,256]{3,1,2,0:T(4,128)S(1)}, u32[]{:S(2)}, u32[]{:S(2)}) collective-permute-start(f32[1,4,64,256]{3,1,2,0:T(4,128)S(1)} %get-tuple-element.19), channel_id=1, source_target_pairs={{0,1},{1,2},{2,3},{3,4},{4,5},{5,6},{6,7},{8,9},{9,10},{10,11},{11... | collective-permute-start | bytes 786440 | tf_op jit(solution)/shard_map/ppermute | solution.py:16
  164.6 19.6 %collective-permute-start.15 = (f32[1,4,64,256]{3,1,2,0:T(4,128)}, f32[1,4,64,256]{3,1,2,0:T(4,128)}, u32[]{:S(2)}, u32[]{:S(2)}) collective-permute-start(f32[1,4,64,256]{3,1,2,0:T(4,128)} %get-tuple-element.22), channel_id=1, source_target_pairs={{1,0},{2,1},{3,2},{4,3},{5,4},{6,5},{7,6},{9,8},{10,9},{11,10},{12... | collective-permute-start | bytes 786440 | tf_op jit(solution)/shard_map/ppermute | solution.py:17
  165.9 18.3 %collective-permute-start.16 = (f32[1,4,64,256]{3,1,2,0:T(4,128)}, f32[1,4,64,256]{3,1,2,0:T(4,128)}, u32[]{:S(2)}, u32[]{:S(2)}) collective-permute-start(f32[1,4,64,256]{3,1,2,0:T(4,128)} %get-tuple-element.23), channel_id=1, source_target_pairs={{0,1},{1,2},{2,3},{3,4},{4,5},{5,6},{6,7},{8,9},{9,10},{10,11},{11... | collective-permute-start | bytes 786440 | tf_op jit(solution)/shard_map/ppermute | solution.py:16
  179.3 28.2 %collective-permute-start.11 = (f32[1,4,64,256]{3,1,2,0:T(4,128)S(1)}, f32[1,4,64,256]{3,1,2,0:T(4,128)S(1)}, u32[]{:S(2)}, u32[]{:S(2)}) collective-permute-start(f32[1,4,64,256]{3,1,2,0:T(4,128)S(1)} %get-tuple-element.14), channel_id=1, source_target_pairs={{1,0},{2,1},{3,2},{4,3},{5,4},{6,5},{7,6},{9,8},{10,9},{11,10},{12... | collective-permute-start | bytes 786440 | tf_op jit(solution)/shard_map/ppermute | solution.py:17
  180.6 26.9 %collective-permute-start.12 = (f32[1,4,64,256]{3,1,2,0:T(4,128)S(1)}, f32[1,4,64,256]{3,1,2,0:T(4,128)S(1)}, u32[]{:S(2)}, u32[]{:S(2)}) collective-permute-start(f32[1,4,64,256]{3,1,2,0:T(4,128)S(1)} %get-tuple-element.15), channel_id=1, source_target_pairs={{0,1},{1,2},{2,3},{3,4},{4,5},{5,6},{6,7},{8,9},{9,10},{10,11},{11... | collective-permute-start | bytes 786440 | tf_op jit(solution)/shard_map/ppermute | solution.py:16
  184.2 25.0 %copy-start.11 = (f32[1,16,64,256]{3,1,2,0:T(8,128)S(1)}, f32[1,16,64,256]{3,1,2,0:T(8,128)}, u32[]{:S(2)}) copy-start(f32[1,16,64,256]{3,1,2,0:T(8,128)} %copy-done.9) | copy-start | bytes 3145732
  184.2 25.0 %copy-start.13 = (f32[1,16,64,256]{3,1,2,0:T(8,128)S(1)}, f32[1,16,64,256]{3,1,2,0:T(8,128)}, u32[]{:S(2)}) copy-start(f32[1,16,64,256]{3,1,2,0:T(8,128)} %copy-done.12) | copy-start | bytes 3145732
  201.9 5.6 %collective-permute-start.17 = (f32[1,4,64,256]{3,1,2,0:T(4,128)S(1)}, f32[1,4,64,256]{3,1,2,0:T(4,128)S(1)}, u32[]{:S(2)}, u32[]{:S(2)}) collective-permute-start(f32[1,4,64,256]{3,1,2,0:T(4,128)S(1)} %get-tuple-element.16), channel_id=1, source_target_pairs={{1,0},{2,1},{3,2},{4,3},{5,4},{6,5},{7,6},{9,8},{10,9},{11,10},{12... | collective-permute-start | bytes 786440 | tf_op jit(solution)/shard_map/ppermute | solution.py:17
  203.2 5.4 %collective-permute-start.18 = (f32[1,4,64,256]{3,1,2,0:T(4,128)S(1)}, f32[1,4,64,256]{3,1,2,0:T(4,128)S(1)}, u32[]{:S(2)}, u32[]{:S(2)}) collective-permute-start(f32[1,4,64,256]{3,1,2,0:T(4,128)S(1)} %get-tuple-element.17), channel_id=1, source_target_pairs={{0,1},{1,2},{2,3},{3,4},{4,5},{5,6},{6,7},{8,9},{9,10},{10,11},{11... | collective-permute-start | bytes 786440 | tf_op jit(solution)/shard_map/ppermute | solution.py:16
  220.9 16.1 %collective-permute-start.19 = (f32[16,64,256]{2,0,1:T(8,128)S(1)}, f32[16,64,256]{2,0,1:T(8,128)S(1)}, u32[]{:S(2)}, u32[]{:S(2)}) collective-permute-start(f32[16,64,256]{2,0,1:T(8,128)S(1)} %fusion.38), channel_id=1, source_target_pairs={{0,1},{1,2},{2,3},{3,4},{4,5},{5,6},{6,7},{7,0},{8,9},{9,10},{10,1... | collective-permute-start | bytes 3145736 | tf_op jit(solution)/shard_map/ppermute | solution.py:25
  237.2 28.9 %collective-permute-start.20 = (f32[16,64,256]{2,0,1:T(8,128)S(1)}, f32[16,64,256]{2,0,1:T(8,128)S(1)}, u32[]{:S(2)}, u32[]{:S(2)}) collective-permute-start(f32[16,64,256]{2,0,1:T(8,128)S(1)} %broadcast_select_fusion.4), channel_id=1, source_target_pairs={{0,2},{1,3},{2,4},{3,5},{4,6},{5,7},{6,0},{7,1},{8,10},{9,11},{10,... | collective-permute-start | bytes 3145736 | tf_op jit(solution)/shard_map/ppermute | solution.py:25
  266.4 45.7 %collective-permute-start.21 = (f32[16,64,256]{2,0,1:T(8,128)S(1)}, f32[16,64,256]{2,0,1:T(8,128)S(1)}, u32[]{:S(2)}, u32[]{:S(2)}) collective-permute-start(f32[16,64,256]{2,0,1:T(8,128)S(1)} %broadcast_select_fusion.6), channel_id=1, source_target_pairs={{0,4},{1,5},{2,6},{3,7},{4,0},{5,1},{6,2},{7,3},{8,12},{9,13},{10,... | collective-permute-start | bytes 3145736 | tf_op jit(solution)/shard_map/ppermute | solution.py:25
  (15 other events, 99.3 us)
Sparse Core Ops, SparseCore 0:
  315.5 35.4 reduce-scatter.4
where the time goes:
time: 361 us; the launch traced here: 360 us
  waiting for transfers between devices  179 us (50%)
  starting transfers between devices  57.9 us (16%)
  other arithmetic  45.9 us (13%)
  matrix products  45.3 us (13%)
  local copies, waits for them, and re-layouts  16.5 us (5%)
  between operations  15.3 us (4%)
    ppermute x6, waiting for transfers between devices, passed_along(): return lax.ppermute(value, axis, pairs)  142 us
    dot_general x4, matrix products, body(): jnp.einsum('srx,sryz->sxyz', weighted, rec_plane, precision=lax.Precision...  45.3 us
    unnamed x2, waiting for transfers between devices  35.7 us
    ppermute x8, starting transfers between devices, extended(): before = lax.ppermute(last, axis, up)  34.4 us
    select_n x3, other arithmetic, body(): jnp.where(active, u_next, u_now)  31.4 us
    ppermute x6, starting transfers between devices, passed_along(): return lax.ppermute(value, axis, pairs)  13.2 us
    ppermute x8, starting transfers between devices, extended(): after = lax.ppermute(leading, axis, down)  10.3 us
    unnamed x52, local copies, waits for them, and re-layouts  7.72 us
  transfers between devices with their start and end apart: 23, of which 8 were waited for; matrix products, arithmetic and copies ran while one was open for 23% of the time, Pallas kernels for 0%

commit v1 on v0

v1 whole, which is shorter than its diff:
```python
import functools

import jax
import jax.numpy as jnp
from jax import lax
from jax.experimental import pallas as pl
from jax.experimental.pallas import tpu as pltpu
from jax.sharding import PartitionSpec as P

COEF = (-205.0 / 72.0, 1.6, -0.2, 8.0 / 315.0, -1.0 / 560.0)
F32 = jnp.float32
BF16 = jnp.bfloat16
MESH = pl.DeviceIdType.MESH
CHUNK = 4
STEPS = 4


def band(size, centre):
    row = lax.broadcasted_iota(jnp.int32, (size, size), 0)
    col = lax.broadcasted_iota(jnp.int32, (size, size), 1)
    gap = jnp.abs(row - col)
    value = jnp.where(gap == 0, centre, 0.0)
    for k in range(1, 5):
        value = jnp.where(gap == k, COEF[k], value)
    high = value.astype(BF16)
    return high, (value - high.astype(F32)).astype(BF16)


def kernel(
    n, groups, tx, ny, nz, recv,
    first_ref, source_ref, wave_ref, count_ref, rec_ref, rect_ref, res_ref,
    courant, fprev, fnow, aprev, anow,
    out_ref,
    u_buf, w_buf, u_old, w_old, e_buf, d_buf, inj, p_buf,
    tiles, staged, landed, img, shared, pieces, acc, firsts, zmat, ymat, smask, rmat,
    load_sem, halo_send, halo_recv, f_send, f_recv, a_send, a_recv, b_send, b_recv,
    x_send, x_recv, i_send, i_recv, g_send, g_recv, o_send, o_recv,
):
    me = lax.axis_index("mp")
    mine = lax.axis_index("shot")
    q = ny // groups
    gx = min(n, tx)
    gz = n // gx
    px, pz = tx // gx, nz // gz
    chunks = tx // CHUNK
    per = n // chunks
    myc = lax.div(me, per)

    def spot(k):
        if gz == 1:
            return pl.ds(k * px, px), pl.ds(0, nz)
        return (
            pl.ds(lax.div(k, gz) * px, px),
            pl.ds(pl.multiple_of(lax.rem(k, gz) * pz, pz), pz),
        )

    def strip(s):
        return pl.ds(pl.multiple_of(s * q, q), q)

    def others(count, own, visit):
        def go(o, carry):
            visit(lax.rem(own + o, count))
            return carry

        lax.fori_loop(1, count, go, 0)

    def loop(count, visit):
        def go(o, carry):
            visit(o)
            return carry

        lax.fori_loop(0, count, go, 0)

    def remote(src, dst, send, recv_, target):
        return pltpu.make_async_remote_copy(
            src_ref=src, dst_ref=dst, send_sem=send, recv_sem=recv_,
            device_id=target, device_id_type=MESH,
        )

    barrier = pltpu.get_barrier_semaphore()
    others(n, me, lambda k: pl.semaphore_signal(
        barrier, inc=1, device_id={"mp": k}, device_id_type=MESH))
    others(groups, mine, lambda s: pl.semaphore_signal(
        barrier, inc=1, device_id={"shot": s}, device_id_type=MESH))
    pl.semaphore_wait(barrier, n - 1 + groups - 1)

    def model_copy(k, sender):
        xs, zs = spot(k)
        return remote(
            courant.at[:, xs, strip(mine), zs], tiles.at[:, sender],
            a_send.at[k], a_recv.at[sender], {"mp": k})

    def first_copy(s, sender):
        return remote(firsts.at[sender], firsts.at[sender], f_send.at[s], f_recv.at[sender], {"shot": s})

    firsts[pl.ds(mine, 1)] = jnp.full((1, 8, 128), first_ref[0], jnp.int32)
    others(groups, mine, lambda s: first_copy(s, mine).start())
    others(n, me, lambda k: model_copy(k, me).start())
    my_x, my_z = spot(me)
    own_tile = pltpu.make_async_copy(
        courant.at[:, my_x, strip(mine), my_z], tiles.at[:, me], load_sem.at[4])
    own_tile.start()

    def halo(f, t, side, src):
        buf = (u_buf, w_buf)[f]
        dst = buf.at[t, pl.ds(0, 4)] if side == 0 else buf.at[t, pl.ds(tx + 4, 4)]
        target = me + 1 if side == 0 else me - 1
        return remote(src, dst, halo_send.at[f, t, side], halo_recv.at[f, t, side], {"mp": target})

    def halo_src(f, t, side):
        if t == 0:
            src = (fnow, anow)[f]
            return src.at[0, pl.ds(tx - 4, 4)] if side == 0 else src.at[0, pl.ds(0, 4)]
        buf = (u_buf, w_buf)[f]
        return buf.at[t, pl.ds(tx, 4)] if side == 0 else buf.at[t, pl.ds(4, 4)]

    def send_halo(f, t):
        @pl.when(me < n - 1)
        def _():
            halo(f, t, 0, halo_src(f, t, 0)).start()

        @pl.when(me > 0)
        def _():
            halo(f, t, 1, halo_src(f, t, 1)).start()

    def wait_halo(f, t):
        @pl.when(me > 0)
        def _():
            halo(f, t, 0, halo_src(f, t, 0)).wait_recv()

        @pl.when(me < n - 1)
        def _():
            halo(f, t, 1, halo_src(f, t, 1)).wait_recv()

    def drain_halo(f, t):
        @pl.when(me < n - 1)
        def _():
            halo(f, t, 0, halo_src(f, t, 0)).wait_send()

        @pl.when(me > 0)
        def _():
            halo(f, t, 1, halo_src(f, t, 1)).wait_send()

    send_halo(0, 0)
    send_halo(1, 0)
    loads = [
        pltpu.make_async_copy(fnow.at[0], u_buf.at[0, pl.ds(4, tx)], load_sem.at[0]),
        pltpu.make_async_copy(anow.at[0], w_buf.at[0, pl.ds(4, tx)], load_sem.at[1]),
        pltpu.make_async_copy(fprev.at[0], u_old, load_sem.at[2]),
        pltpu.make_async_copy(aprev.at[0], w_old, load_sem.at[3]),
    ]
    for copy in loads:
        copy.start()

    edge = jnp.zeros((4, ny, nz), F32)

    @pl.when(me == 0)
    def _():
        for t in range(STEPS):
            u_buf[t, pl.ds(0, 4)] = edge
            w_buf[t, pl.ds(0, 4)] = edge

    @pl.when(me == n - 1)
    def _():
        for t in range(STEPS):
            u_buf[t, pl.ds(tx + 4, 4)] = edge
            w_buf[t, pl.ds(tx + 4, 4)] = edge

    high, low = band(nz, 3.0 * COEF[0])
    zmat[pl.ds(0, nz)] = high
    zmat[pl.ds(nz, nz)] = high
    zmat[pl.ds(2 * nz, nz)] = low
    high, low = band(ny, 0.0)
    ymat[...] = jnp.concatenate([high, high, low], axis=1)
    y_id = lax.broadcasted_iota(jnp.int32, (ny, nz), 0)
    z_id = lax.broadcasted_iota(jnp.int32, (ny, nz), 1)
    smask[...] = jnp.where((y_id == source_ref[0, 1]) & (z_id == source_ref[0, 2]), 1.0, 0.0)
    hit_z = rec_ref[:, 2:3] == lax.broadcasted_iota(jnp.int32, (recv, nz), 1)
    hit_z = jnp.where(hit_z, 1.0, 0.0).astype(BF16)
    for i in range(3):
        rmat[pl.ds(i * recv, recv)] = hit_z
    res = res_ref[...]
    res0 = res.astype(BF16).astype(F32)
    res1 = (res - res0).astype(BF16).astype(F32)
    res2 = res - res0 - res1
    res_all = jnp.concatenate([res0, res1, res2], axis=1)
    rec_all = jnp.concatenate([rect_ref[...]] * 3, axis=1)
    hit_y = lax.broadcasted_iota(jnp.int32, (ny, 3 * recv), 0) == rec_all[1:2]
    hit_y = jnp.where(hit_y, 1.0, 0.0)

    def inject(c):
        x0 = c * CHUNK
        for s in range(STEPS):
            rows = []
            for i in range(CHUNK):
                at_x = jnp.where(rec_all[0:1] == me * tx + x0 + i, res_all[s:s + 1], 0.0)
                rows.append((hit_y * at_x).astype(BF16))
            field = jnp.dot(jnp.concatenate(rows, axis=0), rmat[...], preferred_element_type=F32)
            inj[s, pl.ds(x0, CHUNK)] = field.reshape(CHUNK, ny, nz)

    loop(chunks, inject)

    own_tile.wait()
    others(n, me, lambda k: model_copy(k, k).wait_recv())
    others(groups, mine, lambda s: first_copy(s, s).wait_recv())
    starts = [jnp.max(firsts[s]) for s in range(groups)]

    def pick(m):
        for s in range(groups):
            t = m + starts[s]
            staged[m, s] = tiles[lax.div(t, n), lax.rem(t, n)]

    def spread_copy(m, sender):
        xs, zs = spot(sender)
        return remote(
            staged.at[m], landed.at[:, xs, :, zs],
            b_send.at[m], b_recv.at[sender], {"mp": m})

    def pick_send(m):
        pick(m)
        spread_copy(m, me).start()

    others(n, me, pick_send)
    pick(me)
    keep_own = pltpu.make_async_copy(staged.at[me], landed.at[:, my_x, :, my_z], load_sem.at[5])
    keep_own.start()

    def lap(buf, t, x0):
        centre = buf[t, pl.ds(x0 + 4, CHUNK)].reshape(CHUNK * ny, nz)
        high = centre.astype(BF16)
        low = (centre - high.astype(F32)).astype(BF16)
        along_z = jnp.dot(
            jnp.concatenate([high, low, high], axis=1), zmat[...], preferred_element_type=F32)
        along_y = []
        for i in range(CHUNK):
            rows = slice(i * ny, (i + 1) * ny)
            stack = jnp.concatenate([high[rows], low[rows], high[rows]], axis=0)
            along_y.append(jnp.dot(ymat[...], stack, preferred_element_type=F32))
        total = along_z.reshape(CHUNK, ny, nz) + jnp.stack(along_y)
        for k in range(1, 5):
            total = total + COEF[k] * (
                buf[t, pl.ds(x0 + 4 + k, CHUNK)] + buf[t, pl.ds(x0 + 4 - k, CHUNK)])
        return total

    count = count_ref[0]
    source_x = source_ref[0, 0] - me * tx

    def drive(t, x0):
        total = lap(u_buf, t, x0)
        parts = []
        for i in range(CHUNK):
            amount = jnp.where(source_x == x0 + i, wave_ref[0, t], 0.0)
            parts.append(total[i] + smask[...] * amount)
        total = jnp.stack(parts)
        if t >= 2:
            total = jnp.where(t < count, total, 0.0)
        return total

    def forward(t, x0):
        own = pl.ds(x0, CHUNK)
        mid = pl.ds(x0 + 4, CHUNK)
        if t == 0:
            total, before = d_buf[0, own], u_old[own]
        else:
            total = drive(t, x0)
            d_buf[t, own] = total
            before = u_old[own] if t == 0 else u_buf[t - 1, mid]
        u_buf[t + 1, mid] = 2.0 * u_buf[t, mid] - before + p_buf[own] * total

    def backward(t, x0):
        own = pl.ds(x0, CHUNK)
        mid = pl.ds(x0 + 4, CHUNK)
        s = STEPS - 1 - t
        total = e_buf[own] if t == 0 else lap(w_buf, t, x0) + inj[s, own]
        now = w_buf[t, mid]
        before = w_buf[t - 1, mid] if s + 1 < 2 else w_old[own]
        new = 2.0 * now - before + p_buf[own] * total
        if s >= 2:
            w_old[own] = jnp.where(s < count, now, before)
            new = jnp.where(s < count, new, now)
        return new

    def adjoint(t, x0):
        w_buf[t + 1, pl.ds(x0 + 4, CHUNK)] = backward(t, x0)

    last = tx - CHUNK
    faces = lambda visit: loop(2, lambda i: visit(i * last))
    inner = lambda visit: loop(chunks - 2, lambda i: visit(CHUNK + i * CHUNK))

    for copy in loads:
        copy.wait()

    def early(x0):
        d_buf[0, pl.ds(x0, CHUNK)] = drive(0, x0)
        e_buf[pl.ds(x0, CHUNK)] = lap(w_buf, 0, x0) + inj[STEPS - 1, pl.ds(x0, CHUNK)]

    inner(early)
    wait_halo(0, 0)
    wait_halo(1, 0)
    faces(early)

    def hand_copy(c, s, sender):
        xs = pl.ds(c * CHUNK, CHUNK)
        return remote(
            landed.at[s, xs], p_buf.at[xs, strip(sender)],
            x_send.at[c, s], x_recv.at[c, sender], {"shot": s})

    keep_own.wait()

    def hand(i):
        c = lax.rem(myc - i + chunks, chunks)

        def arrive(j):
            k = c * per + j

            @pl.when(k != me)
            def _():
                spread_copy(k, k).wait_recv()

        loop(per, arrive)
        others(groups, mine, lambda s: hand_copy(c, s, mine).start())
        xs = pl.ds(c * CHUNK, CHUNK)
        p_buf[xs, strip(mine)] = landed[pl.ds(mine, 1), xs].reshape(CHUNK, q, nz)

    loop(chunks, hand)

    def handed(c):
        others(groups, mine, lambda s: hand_copy(c, s, s).wait_recv())

    loop(chunks, handed)

    for t in range(STEPS - 1):
        if t:
            wait_halo(0, t)
        faces(functools.partial(forward, t))
        send_halo(0, t + 1)
        inner(functools.partial(forward, t))
        if t:
            wait_halo(1, t)
        faces(functools.partial(adjoint, t))
        send_halo(1, t + 1)
        inner(functools.partial(adjoint, t))

    def image_copy(c, s, sender):
        xs = pl.ds(c * CHUNK, CHUNK)
        return remote(
            img.at[xs, strip(s)], shared.at[sender, xs],
            i_send.at[c, s], i_recv.at[c, sender], {"shot": s})

    def final(x0):
        own = pl.ds(x0, CHUNK)
        mid = pl.ds(x0 + 4, CHUNK)
        t = STEPS - 1
        new = backward(t, x0) * d_buf[0, own]
        new = new + w_buf[1, mid] * drive(t, x0)
        for k in range(1, t):
            new = new + w_buf[k + 1, mid] * d_buf[t - k, own]
        img[own] = new
        c = lax.div(x0, CHUNK)
        others(groups, mine, lambda s: image_copy(c, s, mine).start())
        shared[pl.ds(mine, 1), own] = img[own, strip(mine)].reshape(1, CHUNK, q, nz)

    inner(final)
    wait_halo(0, STEPS - 1)
    wait_halo(1, STEPS - 1)
    faces(final)

    def piece_copy(k, sender):
        xs, zs = spot(k)
        return remote(
            shared.at[:, xs, :, zs], pieces.at[sender],
            g_send.at[k], g_recv.at[sender], {"mp": k})

    def scatter(x0):
        c = lax.div(x0, CHUNK)
        others(groups, mine, lambda s: image_copy(c, s, s).wait_recv())

        def go(j):
            k = c * per + j

            @pl.when(k != me)
            def _():
                piece_copy(k, me).start()

        loop(per, go)

    inner(scatter)
    faces(scatter)
    keep_piece = pltpu.make_async_copy(shared.at[:, my_x, :, my_z], pieces.at[me], load_sem.at[6])
    keep_piece.start()
    keep_piece.wait()
    others(n, me, lambda k: piece_copy(k, k).wait_recv())

    def out_copy(i, sender):
        xs, zs = spot(sender)
        return remote(
            acc.at[i], out_ref.at[:, xs, :, zs], o_send.at[i], o_recv.at[sender], {"mp": i})

    def total(i):
        for r in range(2):
            value = jnp.zeros((px, q, pz), F32)
            for s in range(groups):
                m = i + r * n - starts[s]
                inside = (m >= 0) & (m < n)
                piece = pieces[jnp.clip(m, 0, n - 1), s]
                value = value + jnp.where(inside, piece, 0.0)
            acc[i, r] = value

    def total_send(i):
        total(i)
        out_copy(i, me).start()

    others(n, me, total_send)
    total(me)
    keep_out = pltpu.make_async_copy(acc.at[me], out_ref.at[:, my_x, :, my_z], load_sem.at[7])
    keep_out.start()
    keep_out.wait()
    others(n, me, lambda k: out_copy(k, k).wait_recv())

    others(groups, mine, lambda s: first_copy(s, mine).wait_send())
    others(n, me, lambda k: model_copy(k, me).wait_send())
    others(n, me, lambda k: spread_copy(k, me).wait_send())
    loop(chunks, lambda c: others(groups, mine, lambda s: hand_copy(c, s, mine).wait_send()))
    loop(chunks, lambda c: others(groups, mine, lambda s: image_copy(c, s, mine).wait_send()))
    others(n, me, lambda k: piece_copy(k, me).wait_send())
    others(n, me, lambda k: out_copy(k, me).wait_send())
    for t in range(STEPS):
        drain_halo(0, t)
        drain_halo(1, t)


def body(
    courant, aperture_first, source_pos, wavelet, receiver_pos, residual, step_count,
    forward_prev, forward_now, adjoint_prev, adjoint_now,
):
    n = lax.axis_size("mp")
    groups = lax.axis_size("shot")
    tx, ny, nz = courant.shape[1:]
    recv = receiver_pos.shape[1]
    q = ny // groups
    gx = min(n, tx)
    gz = n // gx
    px, pz = tx // gx, nz // gz
    chunks = tx // CHUNK
    smem = pl.BlockSpec(memory_space=pltpu.SMEM)
    vmem = pl.BlockSpec(memory_space=pltpu.VMEM)
    hbm = pl.BlockSpec(memory_space=pl.ANY)
    dma = pltpu.SemaphoreType.DMA
    return pl.pallas_call(
        functools.partial(kernel, n, groups, tx, ny, nz, recv),
        out_shape=jax.ShapeDtypeStruct((2, tx, q, nz), F32),
        in_specs=[smem] * 4 + [vmem] * 3 + [hbm] * 5,
        out_specs=vmem,
        scratch_shapes=[
            pltpu.VMEM((STEPS, tx + 8, ny, nz), F32),
            pltpu.VMEM((STEPS, tx + 8, ny, nz), F32),
            pltpu.VMEM((tx, ny, nz), F32),
            pltpu.VMEM((tx, ny, nz), F32),
            pltpu.VMEM((tx, ny, nz), F32),
            pltpu.VMEM((STEPS - 1, tx, ny, nz), F32),
            pltpu.VMEM((STEPS, tx, ny, nz), F32),
            pltpu.VMEM((tx, ny, nz), F32),
            pltpu.VMEM((2, n, px, q, pz), F32),
            pltpu.VMEM((n, groups, px, q, pz), F32),
            pltpu.VMEM((groups, tx, q, nz), F32),
            pltpu.VMEM((tx, ny, nz), F32),
            pltpu.VMEM((groups, tx, q, nz), F32),
            pltpu.VMEM((n, groups, px, q, pz), F32),
            pltpu.VMEM((n, 2, px, q, pz), F32),
            pltpu.VMEM((groups, 8, 128), jnp.int32),
            pltpu.VMEM((3 * nz, nz), BF16),
            pltpu.VMEM((ny, 3 * ny), BF16),
            pltpu.VMEM((ny, nz), F32),
            pltpu.VMEM((3 * recv, nz), BF16),
            dma((8,)),
            dma((2, STEPS, 2)), dma((2, STEPS, 2)),
            dma((groups,)), dma((groups,)),
            dma((n,)), dma((n,)),
            dma((n,)), dma((n,)),
            dma((chunks, groups)), dma((chunks, groups)),
            dma((chunks, groups)), dma((chunks, groups)),
            dma((n,)), dma((n,)),
            dma((n,)), dma((n,)),
        ],
        compiler_params=pltpu.CompilerParams(
            collective_id=0, has_side_effects=True, vmem_limit_bytes=58 * 1024 * 1024),
    )(
        aperture_first, source_pos, wavelet, step_count,
        receiver_pos[0], receiver_pos[0].T, residual[0],
        courant, forward_prev, forward_now, adjoint_prev, adjoint_now,
    )


def solution(mesh):
    return jax.shard_map(
        body,
        mesh=mesh,
        in_specs=(
            P(None, "mp", None, None),
            P("shot"),
            P("shot", None),
            P("shot", None),
            P("shot", None, None),
            P("shot", None, None),
            P("shot"),
            P("shot", "mp", None, None),
            P("shot", "mp", None, None),
            P("shot", "mp", None, None),
            P("shot", "mp", None, None),
        ),
        out_specs=P(None, "mp", "shot", None),
        check_vma=False,
    )
```

time: 361 us -> 115 us (0.32)
  waiting for transfers between devices: 179 us -> 0 us
  Pallas kernels: 0 us -> 108 us
  starting transfers between devices: 57.9 us -> 0 us
  other arithmetic: 45.9 us -> 0 us
  matrix products: 45.3 us -> 0 us
  between operations: 15.3 us -> 1.31 us
  local copies, waits for them, and re-layouts: 16.5 us -> 3.25 us
    ppermute x22 -> x0, waiting for transfers between devices: 144 us -> none  [the longest x6 142 us: passed_along(): return lax.ppermute(value, axis, pairs)]
    pallas_call x0 -> x1, Pallas kernels: none -> 108 us  [body(): pl.pallas_call(functools.partial(kernel, n, groups, tx, ny, nz, recv), ou...]
    ppermute x22 -> x0, starting transfers between devices: 57.9 us -> none  [the longest x8 34.4 us: extended(): before = lax.ppermute(last, axis, up)]
    dot_general x4 -> x0, matrix products: 45.3 us -> none  [body(): jnp.einsum('srx,sryz->sxyz', weighted, rec_plane, precision=lax.Precision...]
    select_n x10 -> x0, other arithmetic: 43.2 us -> none  [the longest x3 31.4 us: body(): jnp.where(active, u_next, u_now)]
    unnamed x2 -> x0, waiting for transfers between devices: 35.7 us -> none
    slice x11 -> x0, local copies, waits for them, and re-layouts: 6.28 us -> none  [the longest x8 3.27 us: extended(): leading = lax.slice_in_dim(value, 0, width, axis=dim)]
    unnamed x52 -> x4, local copies, waits for them, and re-layouts: 7.72 us -> 2.56 us
  transfers between devices with their start and end apart: 23 -> 0, of which waited for: 8 -> 0; matrix products, arithmetic and copies ran while one was open for 23% -> 0% of each run, Pallas kernels for 0% -> 0%
where the time goes in v1:
time: 115 us; the launch traced here: 113 us
  Pallas kernels  108 us (94%)
  local copies, waits for them, and re-layouts  3.25 us (3%)
  between operations  1.31 us (1%)
    pallas_call x1, Pallas kernels, body(): pl.pallas_call(functools.partial(kernel, n, groups, tx, ny, nz, recv), ou...  108 us
    unnamed x4, local copies, waits for them, and re-layouts  2.56 us

profile of v1, /device:TPU:0, one launch (start us, length us, event | category | flops | bytes accessed | tf_op | source)
XLA Modules:
  0.0 113.0 jit_solution(13498965741491139971)
XLA Ops:
  1.3 0.7 copy.16
  2.0 0.0 copy-start
  2.0 0.7 copy.12.rec_ref
  2.7 0.0 copy-done
  2.7 108.4 %shard_map.109 = f32[2,16,16,256]{3,2,1,0:T(8,128)} custom-call(s32[1]{0:T(128)S(6)} %copy.18.first_ref, s32[1,3]{1,0:T(1,128)} %source_ref.1, f32[1,4]{1,0:T(1,128)} %wave_ref.1, s32[1]{0:T(128)S(6)} %copy.19.count_ref, s32[32,3]{1,0:T(8,128)} %copy.12.rec_ref, s32[3,32]{1,0:T(4,128)} %bitcast.8, f32[4,32]{1,0:T(4,128)} %bitcast.9, ...), custom_call_target="tpu_custom_call" | custom-call | tf_op jit(solution)/shard_map/pallas_call | solution.py:449
  111.1 1.9 %copy.20 = f32[2,16,16,256]{3,2,1,0:T(8,128)} copy(f32[2,16,16,256]{3,2,1,0:T(8,128)} %shard_map.109) | data formatting | bytes 1048576
Async XLA Ops:
  2.0 0.7 copy-start

commit v2 on v1

--- a/solution.py
+++ b/solution.py
@@ -13,6 +13,7 @@
 MESH = pl.DeviceIdType.MESH
 CHUNK = 4
 STEPS = 4
+HALVES = 2
 
 
 def band(size, centre):
@@ -28,31 +29,22 @@
 
 def kernel(
     n, groups, tx, ny, nz, recv,
-    first_ref, source_ref, wave_ref, count_ref, rec_ref, rect_ref, res_ref,
+    first_ref, source_ref, wave_ref, count_ref, rec_ref, res_ref,
     courant, fprev, fnow, aprev, anow,
     out_ref,
     u_buf, w_buf, u_old, w_old, e_buf, d_buf, inj, p_buf,
-    tiles, staged, landed, img, shared, pieces, acc, firsts, zmat, ymat, smask, rmat,
+    tiles, staged, img, shared, beside, part, arrived, firsts, zmat, ymat, smask, rmat,
     load_sem, halo_send, halo_recv, f_send, f_recv, a_send, a_recv, b_send, b_recv,
     x_send, x_recv, i_send, i_recv, g_send, g_recv, o_send, o_recv,
 ):
     me = lax.axis_index("mp")
     mine = lax.axis_index("shot")
+    chip, core = lax.div(me, 2), lax.rem(me, 2)
+    sibling = me + 1 - 2 * core
+    line = n // 2
     q = ny // groups
-    gx = min(n, tx)
-    gz = n // gx
-    px, pz = tx // gx, nz // gz
     chunks = tx // CHUNK
-    per = n // chunks
-    myc = lax.div(me, per)
-
-    def spot(k):
-        if gz == 1:
-            return pl.ds(k * px, px), pl.ds(0, nz)
-        return (
-            pl.ds(lax.div(k, gz) * px, px),
-            pl.ds(pl.multiple_of(lax.rem(k, gz) * pz, pz), pz),
-        )
+    half = tx // HALVES
 
     def strip(s):
         return pl.ds(pl.multiple_of(s * q, q), q)
@@ -78,27 +70,73 @@
         )
 
     barrier = pltpu.get_barrier_semaphore()
-    others(n, me, lambda k: pl.semaphore_signal(
-        barrier, inc=1, device_id={"mp": k}, device_id_type=MESH))
+    nearby = [(me - 1, me >= 1), (me + 1, me < n - 1), (me - 2, me >= 2), (me + 2, me < n - 2)]
+    for k, there in nearby:
+        @pl.when(there)
+        def _(k=k):
+            pl.semaphore_signal(barrier, inc=1, device_id={"mp": k}, device_id_type=MESH)
     others(groups, mine, lambda s: pl.semaphore_signal(
         barrier, inc=1, device_id={"shot": s}, device_id_type=MESH))
-    pl.semaphore_wait(barrier, n - 1 + groups - 1)
-
-    def model_copy(k, sender):
-        xs, zs = spot(k)
+    peers = groups - 1 + jnp.minimum(me, 2) + jnp.minimum(n - 1 - me, 2)
+    pl.semaphore_wait(barrier, peers)
+
+    def tile_ref(h, r, z, c):
+        return tiles.at[r, 2 * z + c, pl.ds(h * half, half)]
+
+    def own_ref(h, r):
+        return courant.at[r, pl.ds(h * half, half), strip(mine)]
+
+    def along(h, r, z, src):
         return remote(
-            courant.at[:, xs, strip(mine), zs], tiles.at[:, sender],
-            a_send.at[k], a_recv.at[sender], {"mp": k})
+            src, tile_ref(h, r, z, core), a_send.at[h, r, z], a_recv.at[h, r, z],
+            {"mp": me - 2 if r == 0 else me + 2})
+
+    def across(h, r, z, src, c):
+        return remote(
+            src, tile_ref(h, r, z, c), b_send.at[h, r, z], b_recv.at[h, r, z], {"mp": sibling})
+
+    def onward(r):
+        return chip > 0 if r == 0 else chip < line - 1
+
+    def send_own(h):
+        for r in range(2):
+            @pl.when(onward(r))
+            def _():
+                along(h, r, chip, own_ref(h, r)).start()
+        for r in range(2):
+            across(h, r, chip, own_ref(h, r), core).start()
+
+    def hop(h, d):
+        for r in range(2):
+            z = chip + d if r == 0 else chip - d
+            there = z < line if r == 0 else z >= 0
+
+            @pl.when(there)
+            def _():
+                along(h, r, z, tile_ref(h, r, z, core)).wait_recv()
+
+                @pl.when(onward(r))
+                def _():
+                    along(h, r, z, tile_ref(h, r, z, core)).start()
+
+                across(h, r, z, tile_ref(h, r, z, core), core).start()
+
+    def each_tile(visit):
+        for d in range(line):
+            for r in range(2):
+                z = chip + d if r == 0 else chip - d
+
+                @pl.when(z < line if r == 0 else z >= 0)
+                def _():
+                    visit(r, z)
 
     def first_copy(s, sender):
         return remote(firsts.at[sender], firsts.at[sender], f_send.at[s], f_recv.at[sender], {"shot": s})
 
+    send_own(0)
     firsts[pl.ds(mine, 1)] = jnp.full((1, 8, 128), first_ref[0], jnp.int32)
     others(groups, mine, lambda s: first_copy(s, mine).start())
-    others(n, me, lambda k: model_copy(k, me).start())
-    my_x, my_z = spot(me)
-    own_tile = pltpu.make_async_copy(
-        courant.at[:, my_x, strip(mine), my_z], tiles.at[:, me], load_sem.at[4])
+    own_tile = pltpu.make_async_copy(courant.at[:, :, strip(mine)], tiles.at[:, me], load_sem.at[4])
     own_tile.start()
 
     def halo(f, t, side, src):
@@ -141,8 +179,6 @@
         def _():
             halo(f, t, 1, halo_src(f, t, 1)).wait_send()
 
-    send_halo(0, 0)
-    send_halo(1, 0)
     loads = [
         pltpu.make_async_copy(fnow.at[0], u_buf.at[0, pl.ds(4, tx)], load_sem.at[0]),
         pltpu.make_async_copy(anow.at[0], w_buf.at[0, pl.ds(4, tx)], load_sem.at[1]),
@@ -175,17 +211,21 @@
     y_id = lax.broadcasted_iota(jnp.int32, (ny, nz), 0)
     z_id = lax.broadcasted_iota(jnp.int32, (ny, nz), 1)
     smask[...] = jnp.where((y_id == source_ref[0, 1]) & (z_id == source_ref[0, 2]), 1.0, 0.0)
-    hit_z = rec_ref[:, 2:3] == lax.broadcasted_iota(jnp.int32, (recv, nz), 1)
+    same = (lax.broadcasted_iota(jnp.int32, (recv, recv), 0)
+            == lax.broadcasted_iota(jnp.int32, (recv, recv), 1))
+    at_z = jnp.sum(jnp.where(same, rec_ref[2].astype(F32), 0.0), axis=1, keepdims=True)
+    hit_z = at_z.astype(jnp.int32) == lax.broadcasted_iota(jnp.int32, (recv, nz), 1)
     hit_z = jnp.where(hit_z, 1.0, 0.0).astype(BF16)
     for i in range(3):
         rmat[pl.ds(i * recv, recv)] = hit_z
-    res = res_ref[...]
+    res = res_ref[0]
     res0 = res.astype(BF16).astype(F32)
     res1 = (res - res0).astype(BF16).astype(F32)
     res2 = res - res0 - res1
     res_all = jnp.concatenate([res0, res1, res2], axis=1)
-    rec_all = jnp.concatenate([rect_ref[...]] * 3, axis=1)
-    hit_y = lax.broadcasted_iota(jnp.int32, (ny, 3 * recv), 0) == rec_all[1:2]
+    rec_x = jnp.concatenate([rec_ref[0]] * 3, axis=1)
+    rec_y = jnp.concatenate([rec_ref[1]] * 3, axis=1)
+    hit_y = lax.broadcasted_iota(jnp.int32, (ny, 3 * recv), 0) == rec_y
     hit_y = jnp.where(hit_y, 1.0, 0.0)
 
     def inject(c):
@@ -193,37 +233,58 @@
         for s in range(STEPS):
             rows = []
             for i in range(CHUNK):
-                at_x = jnp.where(rec_all[0:1] == me * tx + x0 + i, res_all[s:s + 1], 0.0)
+                at_x = jnp.where(rec_x == me * tx + x0 + i, res_all[s:s + 1], 0.0)
                 rows.append((hit_y * at_x).astype(BF16))
             field = jnp.dot(jnp.concatenate(rows, axis=0), rmat[...], preferred_element_type=F32)
             inj[s, pl.ds(x0, CHUNK)] = field.reshape(CHUNK, ny, nz)
 
-    loop(chunks, inject)
-
-    own_tile.wait()
-    others(n, me, lambda k: model_copy(k, k).wait_recv())
-    others(groups, mine, lambda s: first_copy(s, s).wait_recv())
-    starts = [jnp.max(firsts[s]) for s in range(groups)]
-
-    def pick(m):
-        for s in range(groups):
-            t = m + starts[s]
-            staged[m, s] = tiles[lax.div(t, n), lax.rem(t, n)]
-
-    def spread_copy(m, sender):
-        xs, zs = spot(sender)
+    def hand_copy(h, s, sender):
+        xs = pl.ds(h * half, half)
         return remote(
-            staged.at[m], landed.at[:, xs, :, zs],
-            b_send.at[m], b_recv.at[sender], {"mp": m})
-
-    def pick_send(m):
-        pick(m)
-        spread_copy(m, me).start()
-
-    others(n, me, pick_send)
-    pick(me)
-    keep_own = pltpu.make_async_copy(staged.at[me], landed.at[:, my_x, :, my_z], load_sem.at[5])
-    keep_own.start()
+            staged.at[s, xs], p_buf.at[xs, strip(sender)],
+            x_send.at[h, s], x_recv.at[h, sender], {"shot": s})
+
+    def picked(s, x):
+        first = jnp.max(firsts[pl.ds(s, 1)])
+        value = jnp.zeros((1, q, nz), F32)
+        for k in range(n + 1):
+            t = me + k
+            value = jnp.where(first == k, tiles[lax.div(t, n), lax.rem(t, n), pl.ds(x, 1)], value)
+        return value
+
+    def hand(h):
+        each_tile(lambda r, z: across(h, r, z, tile_ref(h, r, z, core), 1 - core).wait_recv())
+
+        def give(s):
+            def plane(i):
+                staged[pl.ds(s, 1), pl.ds(h * half + i, 1)] = picked(s, h * half + i)[None]
+
+            loop(half, plane)
+            hand_copy(h, s, mine).start()
+
+        others(groups, mine, give)
+
+        def keep(i):
+            p_buf[pl.ds(h * half + i, 1), strip(mine)] = picked(mine, h * half + i)
+
+        loop(half, keep)
+
+    events = sorted((d + 1.5 * h, h, d) for h in range(HALVES) for d in range(1, line))
+    for i, (when, h, d) in enumerate(events):
+        hop(h, d)
+        if i == 0:
+            for later in range(1, HALVES):
+                send_own(later)
+        if i == len(events) - 2:
+            send_halo(0, 0)
+            send_halo(1, 0)
+        if i < chunks:
+            inject(i)
+        if d == line - 1:
+            if h == 0:
+                own_tile.wait()
+                others(groups, mine, lambda s: first_copy(s, s).wait_recv())
+            hand(h)
 
     def lap(buf, t, x0):
         centre = buf[t, pl.ds(x0 + 4, CHUNK)].reshape(CHUNK * ny, nz)
@@ -299,35 +360,8 @@
     wait_halo(1, 0)
     faces(early)
 
-    def hand_copy(c, s, sender):
-        xs = pl.ds(c * CHUNK, CHUNK)
-        return remote(
-            landed.at[s, xs], p_buf.at[xs, strip(sender)],
-            x_send.at[c, s], x_recv.at[c, sender], {"shot": s})
-
-    keep_own.wait()
-
-    def hand(i):
-        c = lax.rem(myc - i + chunks, chunks)
-
-        def arrive(j):
-            k = c * per + j
-
-            @pl.when(k != me)
-            def _():
-                spread_copy(k, k).wait_recv()
-
-        loop(per, arrive)
-        others(groups, mine, lambda s: hand_copy(c, s, mine).start())
-        xs = pl.ds(c * CHUNK, CHUNK)
-        p_buf[xs, strip(mine)] = landed[pl.ds(mine, 1), xs].reshape(CHUNK, q, nz)
-
-    loop(chunks, hand)
-
-    def handed(c):
-        others(groups, mine, lambda s: hand_copy(c, s, s).wait_recv())
-
-    loop(chunks, handed)
+    for h in range(HALVES):
+        others(groups, mine, lambda s: hand_copy(h, s, s).wait_recv())
 
     for t in range(STEPS - 1):
         if t:
@@ -365,65 +399,88 @@
     wait_halo(1, STEPS - 1)
     faces(final)
 
-    def piece_copy(k, sender):
-        xs, zs = spot(k)
+    def beside_copy(c):
+        xs = pl.ds(c * CHUNK, CHUNK)
+        return remote(shared.at[:, xs], beside.at[:, xs], g_send.at[c], g_recv.at[c], {"mp": sibling})
+
+    order = list(range(1, chunks - 1)) + [0, chunks - 1]
+    for c in order:
+        others(groups, mine, lambda s: image_copy(c, s, s).wait_recv())
+        beside_copy(c).start()
+
+    starts = [jnp.max(firsts[s]) for s in range(groups)]
+
+    def sum_copy(r, z, c):
+        xs = pl.ds(c * CHUNK, CHUNK)
         return remote(
-            shared.at[:, xs, :, zs], pieces.at[sender],
-            g_send.at[k], g_recv.at[sender], {"mp": k})
-
-    def scatter(x0):
-        c = lax.div(x0, CHUNK)
-        others(groups, mine, lambda s: image_copy(c, s, s).wait_recv())
-
-        def go(j):
-            k = c * per + j
-
-            @pl.when(k != me)
+            part.at[r, z, xs], arrived.at[r, z, xs], o_send.at[r, z, c], o_recv.at[r, z, c],
+            {"mp": me + 2 if r == 0 else me - 2})
+
+    def local_sum(r, z, c):
+        tile = r * n + 2 * z + core
+        xs = pl.ds(c * CHUNK, CHUNK)
+        value = jnp.zeros((CHUNK, q, nz), F32)
+        for s in range(groups):
+            value = value + jnp.where(starts[s] == tile - me, shared[s, xs], 0.0)
+            value = value + jnp.where(starts[s] == tile - sibling, beside[s, xs], 0.0)
+        return value
+
+    def sourced(r):
+        return chip > 0 if r == 0 else chip < line - 1
+
+    for j in range(line - 1):
+        for c in order:
+            if j == 0:
+                beside_copy(c).wait_recv()
+            xs = pl.ds(c * CHUNK, CHUNK)
+            for r in range(2):
+                late = chip if r == 0 else line - 1 - chip
+                z = line - 1 - j + chip if r == 0 else j - line + 1 + chip
+
+                @pl.when(late <= j)
+                def _():
+                    part[r, z, xs] = local_sum(r, z, c)
+
+                    @pl.when(sourced(r))
+                    def _():
+                        sum_copy(r, z, c).wait_recv()
+                        part[r, z, xs] += arrived[r, z, xs]
+
+                    sum_copy(r, z, c).start()
+
+    for c in order:
+        xs = pl.ds(c * CHUNK, CHUNK)
+        for r in range(2):
+            out_ref[r, xs] = local_sum(r, chip, c)
+
+            @pl.when(sourced(r))
             def _():
-                piece_copy(k, me).start()
-
-        loop(per, go)
-
-    inner(scatter)
-    faces(scatter)
-    keep_piece = pltpu.make_async_copy(shared.at[:, my_x, :, my_z], pieces.at[me], load_sem.at[6])
-    keep_piece.start()
-    keep_piece.wait()
-    others(n, me, lambda k: piece_copy(k, k).wait_recv())
-
-    def out_copy(i, sender):
-        xs, zs = spot(sender)
-        return remote(
-            acc.at[i], out_ref.at[:, xs, :, zs], o_send.at[i], o_recv.at[sender], {"mp": i})
-
-    def total(i):
-        for r in range(2):
-            value = jnp.zeros((px, q, pz), F32)
-            for s in range(groups):
-                m = i + r * n - starts[s]
-                inside = (m >= 0) & (m < n)
-                piece = pieces[jnp.clip(m, 0, n - 1), s]
-                value = value + jnp.where(inside, piece, 0.0)
-            acc[i, r] = value
-
-    def total_send(i):
-        total(i)
-        out_copy(i, me).start()
-
-    others(n, me, total_send)
-    total(me)
-    keep_out = pltpu.make_async_copy(acc.at[me], out_ref.at[:, my_x, :, my_z], load_sem.at[7])
-    keep_out.start()
-    keep_out.wait()
-    others(n, me, lambda k: out_copy(k, k).wait_recv())
+                sum_copy(r, chip, c).wait_recv()
+                out_ref[r, xs] += arrived[r, chip, xs]
 
     others(groups, mine, lambda s: first_copy(s, mine).wait_send())
-    others(n, me, lambda k: model_copy(k, me).wait_send())
-    others(n, me, lambda k: spread_copy(k, me).wait_send())
-    loop(chunks, lambda c: others(groups, mine, lambda s: hand_copy(c, s, mine).wait_send()))
-    loop(chunks, lambda c: others(groups, mine, lambda s: image_copy(c, s, mine).wait_send()))
-    others(n, me, lambda k: piece_copy(k, me).wait_send())
-    others(n, me, lambda k: out_copy(k, me).wait_send())
+    for h in range(HALVES):
+        def sent(r, z):
+            src = tile_ref(h, r, z, core)
+            across(h, r, z, src, core).wait_send()
+
+            @pl.when(onward(r))
+            def _():
+                along(h, r, z, src).wait_send()
+
+        each_tile(sent)
+        others(groups, mine, lambda s: hand_copy(h, s, mine).wait_send())
+    for c in range(chunks):
+        others(groups, mine, lambda s: image_copy(c, s, mine).wait_send())
+        beside_copy(c).wait_send()
+        for j in range(line - 1):
+            for r in range(2):
+                late = chip if r == 0 else line - 1 - chip
+                z = line - 1 - j + chip if r == 0 else j - line + 1 + chip
+
+                @pl.when(late <= j)
+                def _():
+                    sum_copy(r, z, c).wait_send()
     for t in range(STEPS):
         drain_halo(0, t)
         drain_halo(1, t)
@@ -438,9 +495,7 @@
     tx, ny, nz = courant.shape[1:]
     recv = receiver_pos.shape[1]
     q = ny // groups
-    gx = min(n, tx)
-    gz = n // gx
-    px, pz = tx // gx, nz // gz
+    line = n // 2
     chunks = tx // CHUNK
     smem = pl.BlockSpec(memory_space=pltpu.SMEM)
     vmem = pl.BlockSpec(memory_space=pltpu.VMEM)
@@ -449,7 +504,7 @@
     return pl.pallas_call(
         functools.partial(kernel, n, groups, tx, ny, nz, recv),
         out_shape=jax.ShapeDtypeStruct((2, tx, q, nz), F32),
-        in_specs=[smem] * 4 + [vmem] * 3 + [hbm] * 5,
+        in_specs=[smem] * 4 + [vmem] * 2 + [hbm] * 5,
         out_specs=vmem,
         scratch_shapes=[
             pltpu.VMEM((STEPS, tx + 8, ny, nz), F32),
@@ -460,33 +515,33 @@
             pltpu.VMEM((STEPS - 1, tx, ny, nz), F32),
             pltpu.VMEM((STEPS, tx, ny, nz), F32),
             pltpu.VMEM((tx, ny, nz), F32),
-            pltpu.VMEM((2, n, px, q, pz), F32),
-            pltpu.VMEM((n, groups, px, q, pz), F32),
+            pltpu.VMEM((2, n, tx, q, nz), F32),
             pltpu.VMEM((groups, tx, q, nz), F32),
             pltpu.VMEM((tx, ny, nz), F32),
             pltpu.VMEM((groups, tx, q, nz), F32),
-            pltpu.VMEM((n, groups, px, q, pz), F32),
-            pltpu.VMEM((n, 2, px, q, pz), F32),
+            pltpu.VMEM((groups, tx, q, nz), F32),
+            pltpu.VMEM((2, line, tx, q, nz), F32),
+            pltpu.VMEM((2, line, tx, q, nz), F32),
             pltpu.VMEM((groups, 8, 128), jnp.int32),
             pltpu.VMEM((3 * nz, nz), BF16),
             pltpu.VMEM((ny, 3 * ny), BF16),
             pltpu.VMEM((ny, nz), F32),
             pltpu.VMEM((3 * recv, nz), BF16),
-            dma((8,)),
+            dma((5,)),
             dma((2, STEPS, 2)), dma((2, STEPS, 2)),
             dma((groups,)), dma((groups,)),
-            dma((n,)), dma((n,)),
-            dma((n,)), dma((n,)),
+            dma((HALVES, 2, line)), dma((HALVES, 2, line)),
+            dma((HALVES, 2, line)), dma((HALVES, 2, line)),
+            dma((HALVES, groups)), dma((HALVES, groups)),
             dma((chunks, groups)), dma((chunks, groups)),
-            dma((chunks, groups)), dma((chunks, groups)),
-            dma((n,)), dma((n,)),
-            dma((n,)), dma((n,)),
+            dma((chunks,)), dma((chunks,)),
+            dma((2, line, chunks)), dma((2, line, chunks)),
         ],
         compiler_params=pltpu.CompilerParams(
             collective_id=0, has_side_effects=True, vmem_limit_bytes=58 * 1024 * 1024),
     )(
         aperture_first, source_pos, wavelet, step_count,
-        receiver_pos[0], receiver_pos[0].T, residual[0],
+        receiver_pos.transpose(2, 0, 1), residual,
         courant, forward_prev, forward_now, adjoint_prev, adjoint_now,
     )
 

time: 115 us -> 91 us (0.79); the launches traced: 113 us -> 90.8 us
  Pallas kernels: 108 us -> 87.6 us
  local copies, waits for them, and re-layouts: 3.25 us -> 1.87 us
    pallas_call x1, Pallas kernels: 108 us -> 87.6 us  [body(): pl.pallas_call(functools.partial(kernel, n, groups, tx, ny, nz, recv), ou...]
    unnamed x4 -> x1, local copies, waits for them, and re-layouts: 2.56 us -> 1.87 us
where the time goes in v2:
time: 91 us; the launch traced here: 90.8 us
  Pallas kernels  87.6 us (96%)
  local copies, waits for them, and re-layouts  1.87 us (2%)
  between operations  1.3 us (1%)
    pallas_call x1, Pallas kernels, body(): pl.pallas_call(functools.partial(kernel, n, groups, tx, ny, nz, recv), ou...  87.6 us
    unnamed x1, local copies, waits for them, and re-layouts  1.87 us

profile of v2, /device:TPU:0, one launch (start us, length us, event | category | flops | bytes accessed | tf_op | source)
XLA Modules:
  0.0 90.8 jit_solution(16371079984242359421)
XLA Ops:
  1.3 87.6 %shard_map.109 = f32[2,16,16,256]{3,2,1,0:T(8,128)} custom-call(s32[1]{0:T(128)S(6)} %copy.13.first_ref, s32[1,3]{1,0:T(1,128)} %source_ref.1, f32[1,4]{1,0:T(1,128)} %wave_ref.1, s32[1]{0:T(128)S(6)} %copy.14.count_ref, s32[3,1,32]{2,1,0:T(1,128)} %bitcast.1, f32[1,4,32]{2,1,0:T(4,128)} %res_ref.1, f32[2,16,64,256]{3,2,1,0:T(8,128)} %courant.1, ...), custom_call_target="tpu_custom_call" | custom-call | tf_op jit(solution)/shard_map/pallas_call | solution.py:504
  88.9 1.9 %copy.15 = f32[2,16,16,256]{3,2,1,0:T(8,128)} copy(f32[2,16,16,256]{3,2,1,0:T(8,128)} %shard_map.109) | data formatting | bytes 1048576

commit v3 on v2

--- a/solution.py
+++ b/solution.py
@@ -13,18 +13,22 @@
 MESH = pl.DeviceIdType.MESH
 CHUNK = 4
 STEPS = 4
-HALVES = 2
-
-
-def band(size, centre):
+SCALE = 5040.0
+OUTER = (8064.0, -1008.0, 128.0, -9.0)
+
+
+def parts_of(line):
+    return 4 if line <= 4 else 2
+
+
+def band(size):
     row = lax.broadcasted_iota(jnp.int32, (size, size), 0)
     col = lax.broadcasted_iota(jnp.int32, (size, size), 1)
     gap = jnp.abs(row - col)
-    value = jnp.where(gap == 0, centre, 0.0)
+    value = jnp.zeros((size, size), F32)
     for k in range(1, 5):
-        value = jnp.where(gap == k, COEF[k], value)
-    high = value.astype(BF16)
-    return high, (value - high.astype(F32)).astype(BF16)
+        value = jnp.where(gap == k, OUTER[k - 1], value)
+    return value.astype(BF16)
 
 
 def kernel(
@@ -44,7 +48,8 @@
     line = n // 2
     q = ny // groups
     chunks = tx // CHUNK
-    half = tx // HALVES
+    halves = parts_of(line)
+    half = tx // halves
 
     def strip(s):
         return pl.ds(pl.multiple_of(s * q, q), q)
@@ -202,12 +207,13 @@
             u_buf[t, pl.ds(tx + 4, 4)] = edge
             w_buf[t, pl.ds(tx + 4, 4)] = edge
 
-    high, low = band(nz, 3.0 * COEF[0])
-    zmat[pl.ds(0, nz)] = high
-    zmat[pl.ds(nz, nz)] = high
-    zmat[pl.ds(2 * nz, nz)] = low
-    high, low = band(ny, 0.0)
-    ymat[...] = jnp.concatenate([high, high, low], axis=1)
+    band_z, band_y = band(nz), band(ny)
+    zmat[pl.ds(0, nz)] = band_z
+    zmat[pl.ds(nz, nz)] = band_z
+    blank = jnp.zeros((ny, 2 * ny), BF16)
+    pair = jnp.concatenate([band_y, band_y], axis=1)
+    ymat[pl.ds(0, ny)] = jnp.concatenate([pair, blank], axis=1)
+    ymat[pl.ds(ny, ny)] = jnp.concatenate([blank, pair], axis=1)
     y_id = lax.broadcasted_iota(jnp.int32, (ny, nz), 0)
     z_id = lax.broadcasted_iota(jnp.int32, (ny, nz), 1)
     smask[...] = jnp.where((y_id == source_ref[0, 1]) & (z_id == source_ref[0, 2]), 1.0, 0.0)
@@ -269,12 +275,11 @@
 
         loop(half, keep)
 
-    events = sorted((d + 1.5 * h, h, d) for h in range(HALVES) for d in range(1, line))
+    events = sorted((d + (1 + halves / 4) * h, h, d) for h in range(halves) for d in range(1, line))
     for i, (when, h, d) in enumerate(events):
         hop(h, d)
-        if i == 0:
-            for later in range(1, HALVES):
-                send_own(later)
+        if d == 1 and h + 1 < halves:
+            send_own(h + 1)
         if i == len(events) - 2:
             send_halo(0, 0)
             send_halo(1, 0)
@@ -290,14 +295,15 @@
         centre = buf[t, pl.ds(x0 + 4, CHUNK)].reshape(CHUNK * ny, nz)
         high = centre.astype(BF16)
         low = (centre - high.astype(F32)).astype(BF16)
-        along_z = jnp.dot(
-            jnp.concatenate([high, low, high], axis=1), zmat[...], preferred_element_type=F32)
+        outer = jnp.dot(
+            jnp.concatenate([high, low], axis=1), zmat[...], preferred_element_type=F32)
         along_y = []
-        for i in range(CHUNK):
-            rows = slice(i * ny, (i + 1) * ny)
-            stack = jnp.concatenate([high[rows], low[rows], high[rows]], axis=0)
+        for i in range(0, CHUNK, 2):
+            one, two = slice(i * ny, (i + 1) * ny), slice((i + 1) * ny, (i + 2) * ny)
+            stack = jnp.concatenate([high[one], low[one], high[two], low[two]], axis=0)
             along_y.append(jnp.dot(ymat[...], stack, preferred_element_type=F32))
-        total = along_z.reshape(CHUNK, ny, nz) + jnp.stack(along_y)
+        outer = outer + jnp.concatenate(along_y, axis=0)
+        total = (outer * (1.0 / SCALE) + 3.0 * COEF[0] * centre).reshape(CHUNK, ny, nz)
         for k in range(1, 5):
             total = total + COEF[k] * (
                 buf[t, pl.ds(x0 + 4 + k, CHUNK)] + buf[t, pl.ds(x0 + 4 - k, CHUNK)])
@@ -360,7 +366,7 @@
     wait_halo(1, 0)
     faces(early)
 
-    for h in range(HALVES):
+    for h in range(halves):
         others(groups, mine, lambda s: hand_copy(h, s, s).wait_recv())
 
     for t in range(STEPS - 1):
@@ -404,10 +410,6 @@
         return remote(shared.at[:, xs], beside.at[:, xs], g_send.at[c], g_recv.at[c], {"mp": sibling})
 
     order = list(range(1, chunks - 1)) + [0, chunks - 1]
-    for c in order:
-        others(groups, mine, lambda s: image_copy(c, s, s).wait_recv())
-        beside_copy(c).start()
-
     starts = [jnp.max(firsts[s]) for s in range(groups)]
 
     def sum_copy(r, z, c):
@@ -428,11 +430,12 @@
     def sourced(r):
         return chip > 0 if r == 0 else chip < line - 1
 
-    for j in range(line - 1):
-        for c in order:
-            if j == 0:
-                beside_copy(c).wait_recv()
-            xs = pl.ds(c * CHUNK, CHUNK)
+    for c in order:
+        others(groups, mine, lambda s: image_copy(c, s, s).wait_recv())
+        beside_copy(c).start()
+        beside_copy(c).wait_recv()
+        xs = pl.ds(c * CHUNK, CHUNK)
+        for j in range(line - 1):
             for r in range(2):
                 late = chip if r == 0 else line - 1 - chip
                 z = line - 1 - j + chip if r == 0 else j - line + 1 + chip
@@ -447,19 +450,19 @@
                         part[r, z, xs] += arrived[r, z, xs]
 
                     sum_copy(r, z, c).start()
+        for r in range(2):
+            out_ref[r, xs] = local_sum(r, chip, c)
 
     for c in order:
         xs = pl.ds(c * CHUNK, CHUNK)
         for r in range(2):
-            out_ref[r, xs] = local_sum(r, chip, c)
-
             @pl.when(sourced(r))
             def _():
                 sum_copy(r, chip, c).wait_recv()
                 out_ref[r, xs] += arrived[r, chip, xs]
 
     others(groups, mine, lambda s: first_copy(s, mine).wait_send())
-    for h in range(HALVES):
+    for h in range(halves):
         def sent(r, z):
             src = tile_ref(h, r, z, core)
             across(h, r, z, src, core).wait_send()
@@ -496,6 +499,7 @@
     recv = receiver_pos.shape[1]
     q = ny // groups
     line = n // 2
+    halves = parts_of(line)
     chunks = tx // CHUNK
     smem = pl.BlockSpec(memory_space=pltpu.SMEM)
     vmem = pl.BlockSpec(memory_space=pltpu.VMEM)
@@ -523,16 +527,16 @@
             pltpu.VMEM((2, line, tx, q, nz), F32),
             pltpu.VMEM((2, line, tx, q, nz), F32),
             pltpu.VMEM((groups, 8, 128), jnp.int32),
-            pltpu.VMEM((3 * nz, nz), BF16),
-            pltpu.VMEM((ny, 3 * ny), BF16),
+            pltpu.VMEM((2 * nz, nz), BF16),
+            pltpu.VMEM((2 * ny, 4 * ny), BF16),
             pltpu.VMEM((ny, nz), F32),
             pltpu.VMEM((3 * recv, nz), BF16),
             dma((5,)),
             dma((2, STEPS, 2)), dma((2, STEPS, 2)),
             dma((groups,)), dma((groups,)),
-            dma((HALVES, 2, line)), dma((HALVES, 2, line)),
-            dma((HALVES, 2, line)), dma((HALVES, 2, line)),
-            dma((HALVES, groups)), dma((HALVES, groups)),
+            dma((halves, 2, line)), dma((halves, 2, line)),
+            dma((halves, 2, line)), dma((halves, 2, line)),
+            dma((halves, groups)), dma((halves, groups)),
             dma((chunks, groups)), dma((chunks, groups)),
             dma((chunks,)), dma((chunks,)),
             dma((2, line, chunks)), dma((2, line, chunks)),

time: 91 us -> 102 us (1.12)
  Pallas kernels: 87.6 us -> 98.4 us
    pallas_call x1, Pallas kernels: 87.6 us -> 98.4 us  [body(): pl.pallas_call(functools.partial(kernel, n, groups, tx, ny, nz, recv), ou...]
where the time goes in v3:
time: 102 us
  Pallas kernels  98.4 us (96%)
  local copies, waits for them, and re-layouts  1.87 us (2%)
  between operations  1.3 us (1%)
    pallas_call x1, Pallas kernels, body(): pl.pallas_call(functools.partial(kernel, n, groups, tx, ny, nz, recv), ou...  98.4 us

profile of v3, /device:TPU:0, one launch (start us, length us, event | category | flops | bytes accessed | tf_op | source)
XLA Modules:
  0.0 101.6 jit_solution(8830334259025035612)
XLA Ops:
  1.3 98.4 %shard_map.109 = f32[2,16,16,256]{3,2,1,0:T(8,128)} custom-call(s32[1]{0:T(128)S(6)} %copy.13.first_ref, s32[1,3]{1,0:T(1,128)} %source_ref.1, f32[1,4]{1,0:T(1,128)} %wave_ref.1, s32[1]{0:T(128)S(6)} %copy.14.count_ref, s32[3,1,32]{2,1,0:T(1,128)} %bitcast.1, f32[1,4,32]{2,1,0:T(4,128)} %res_ref.1, f32[2,16,64,256]{3,2,1,0:T(8,128)} %courant.1, ...), custom_call_target="tpu_custom_call" | custom-call | tf_op jit(solution)/shard_map/pallas_call | solution.py:508
  99.7 1.9 %copy.15 = f32[2,16,16,256]{3,2,1,0:T(8,128)} copy(f32[2,16,16,256]{3,2,1,0:T(8,128)} %shard_map.109) | data formatting | bytes 1048576
